TPU v7x, 32 devices: a whole 2x2x4 slice. The times are simulated.
32 devices in a mesh: mesh: 16 (over z, y, x), panel: 2 (over core).
Axes of the slice: x: 2, y: 2, z: 4, core: 2. Of those that a mesh axis runs over, the one named last changes fastest.
Arguments:
- basis_vectors: bfloat16 [128, 128, 192], P('mesh', 'panel'), may hold values from -1 to 1
- stiffness_blocks: bfloat16 [896, 192, 192], P('mesh'), may hold values from -0.21875 to 0.21875
- block_rows: int32 [896], P('mesh'), may hold values from 0 to 7
- block_columns: int32 [896], P('mesh'), may hold values from 0 to 23
- density: float32 [896], P('mesh'), may hold values from 0.1 to 1
- block_counts: int32 [16], P('mesh'), may hold values from 14 to 56, as said below
- send_list: int32 [256], P('mesh'), may hold values from 0 to 7
Outputs:
- reduced: float32 [128, 128], P('panel', 'mesh')
Inputs may be any that keep to these rules, and one draw needn't show every extreme that they name: `block_counts`: in every draw some partition holds exactly 56 and another exactly 14.
All inputs are finite; a program needn't handle non-finite values.
Results may differ from a plain program's by a relative error of at most 0.0029.
Values may be sent and summed in bfloat16 or wider, within the bound.
A program may use at most 64 MiB of HBM per device.

v0:
```python
import jax
import jax.numpy as jnp
from jax import lax
from jax.sharding import PartitionSpec as P

GMAX = 4


neighbour_offsets = (1, -1, 2, -2)


def passed_along(block, axis, distance):
    devices = range(lax.axis_size(axis))
    route = [((i - distance) % len(devices), i) for i in devices]
    return lax.ppermute(block, axis, route)


def group_term(source_pool, blocks_here, rows_here, columns, scale, clusters):
    sources = source_pool[columns]
    product = jnp.einsum("bpj,bij->bpi", sources, blocks_here, preferred_element_type=jnp.float32)
    selector = (rows_here[None, :] == jnp.arange(clusters, dtype=jnp.int32)[:, None]).astype(
        jnp.float32
    ) * scale[None, :]
    return jnp.dot(selector, product.reshape(product.shape[0], -1), precision=lax.Precision.HIGHEST)


def local(
    basis_vectors, stiffness_blocks, block_rows, block_columns, density, block_counts, send_list
):
    clusters, panel_width, cluster_dofs = basis_vectors.shape
    capacity = stiffness_blocks.shape[0]
    arriving = []
    for neighbour, offset in enumerate(neighbour_offsets):
        listed = send_list[neighbour * GMAX : (neighbour + 1) * GMAX]
        picked = basis_vectors[listed]
        arriving.append(passed_along(picked, "mesh", offset))
    source_pool = jnp.concatenate([basis_vectors] + arriving, axis=0)
    active = jnp.arange(capacity, dtype=jnp.int32) < block_counts[0]
    scale = jnp.where(active, 0.001 + density**3, jnp.float32(0.0))
    summed = group_term(source_pool, stiffness_blocks, block_rows, block_columns, scale, clusters)
    products = summed.reshape(clusters, panel_width, cluster_dofs).astype(jnp.bfloat16)
    gathered = lax.all_gather(products, "panel", axis=1, tiled=True)
    partial_tile = jnp.einsum(
        "npc,nqc->pq", basis_vectors, gathered, preferred_element_type=jnp.float32
    )
    return lax.psum_scatter(partial_tile, "mesh", scatter_dimension=1, tiled=True)


def solution(mesh):
    placed = (
        P("mesh", "panel", None),
        P("mesh", None, None),
        P("mesh"),
        P("mesh"),
        P("mesh"),
        P("mesh"),
        P("mesh"),
    )
    return jax.shard_map(
        local, mesh=mesh, in_specs=placed, out_specs=P("panel", "mesh"), check_vma=False
    )
```

profile of v0, /device:TPU:0, one launch (start us, length us, event | category | flops | bytes accessed | tf_op | source)
XLA Modules:
  0.0 119.4 jit_solution(14694424376637121011)
XLA Ops:
  0.0 0.9 compare_select_fusion.1
  0.9 1.5 %gather_fusion = bf16[4,64,192]{2,1,0:T(8,128)(2,1)S(1)} fusion(bf16[8,64,192]{2,1,0:T(8,128)(2,1)} %param.7, s32[1024]{0:T(1024)S(1)} %pad_clamp_fusion.4), kind=kCustom, calls=%fused_computation | custom fusion | bytes 196624 | tf_op jit(solution)/shard_map/gather | solution.py:35
  2.4 3.0 %collective-permute-start = (bf16[4,64,192]{2,1,0:T(8,128)(2,1)S(1)}, bf16[4,64,192]{2,1,0:T(8,128)(2,1)S(1)}, u32[]{:S(2)}, u32[]{:S(2)}) collective-permute-start(bf16[4,64,192]{2,1,0:T(8,128)(2,1)S(1)} %gather_fusion), channel_id=1, source_target_pairs={{30,0},{0,2},{2,4},{4,6},{6,8},{8,10},{10,12},{12,14},{14,16},{16,... | collective-permute-start | bytes 294920 | tf_op jit(solution)/shard_map/ppermute | solution.py:15
  5.4 1.5 %gather_fusion.1 = bf16[4,64,192]{2,1,0:T(8,128)(2,1)S(1)} fusion(bf16[8,64,192]{2,1,0:T(8,128)(2,1)} %param.7, s32[1024]{0:T(1024)S(1)} %pad_clamp_fusion.3), kind=kCustom, calls=%fused_computation.1 | custom fusion | bytes 196624 | tf_op jit(solution)/shard_map/gather | solution.py:35
  6.9 4.1 %collective-permute-start.1 = (bf16[4,64,192]{2,1,0:T(8,128)(2,1)S(1)}, bf16[4,64,192]{2,1,0:T(8,128)(2,1)S(1)}, u32[]{:S(2)}, u32[]{:S(2)}) collective-permute-start(bf16[4,64,192]{2,1,0:T(8,128)(2,1)S(1)} %gather_fusion.1), channel_id=1, source_target_pairs={{2,0},{4,2},{6,4},{8,6},{10,8},{12,10},{14,12},{16,14},{18,16},{20... | collective-permute-start | bytes 294920 | tf_op jit(solution)/shard_map/ppermute | solution.py:15
  11.0 1.5 %gather_fusion.2 = bf16[4,64,192]{2,1,0:T(8,128)(2,1)S(1)} fusion(bf16[8,64,192]{2,1,0:T(8,128)(2,1)} %param.7, s32[1024]{0:T(1024)S(1)} %pad_clamp_fusion.2), kind=kCustom, calls=%fused_computation.2 | custom fusion | bytes 196624 | tf_op jit(solution)/shard_map/gather | solution.py:35
  12.5 0.1 collective-permute-start.2
  12.6 1.5 %gather_fusion.3 = bf16[4,64,192]{2,1,0:T(8,128)(2,1)S(1)} fusion(bf16[8,64,192]{2,1,0:T(8,128)(2,1)} %param.7, s32[1024]{0:T(1024)S(1)} %pad_clamp_fusion.1), kind=kCustom, calls=%fused_computation.3 | custom fusion | bytes 196624 | tf_op jit(solution)/shard_map/gather | solution.py:35
  14.1 4.8 %collective-permute-start.3 = (bf16[4,64,192]{2,1,0:T(8,128)(2,1)S(1)}, bf16[4,64,192]{2,1,0:T(8,128)(2,1)S(1)}, u32[]{:S(2)}, u32[]{:S(2)}) collective-permute-start(bf16[4,64,192]{2,1,0:T(8,128)(2,1)S(1)} %gather_fusion.3), channel_id=1, source_target_pairs={{4,0},{6,2},{8,4},{10,6},{12,8},{14,10},{16,12},{18,14},{20,16},{2... | collective-permute-start | bytes 294920 | tf_op jit(solution)/shard_map/ppermute | solution.py:15
  18.8 1.0 constant_dynamic-update-slice_fusion.4
  19.8 0.7 compare_select_fusion
  21.1 0.7 compare_select_fusion.5
  21.8 1.2 %dynamic-slice = u32[1]{0:T(128)} dynamic-slice(u32[32]{0:T(128)} %constant.20, u32[]{:T(128)S(6)} %add.35), dynamic_slice_sizes={1} | dynamic-slice | bytes 12
  23.7 0.0 collective-permute-done
  23.7 0.0 collective-permute-done.1
  23.8 0.0 collective-permute-done.2
  23.8 0.0 collective-permute-done.3
  23.8 0.7 gather_fusion.4
  24.5 6.2 %fusion.9 = f32[56,64,192]{2,1,0:T(8,128)} fusion(bf16[56,64,192]{2,1,0:T(8,128)(2,1)S(1)} %gather_fusion.4, bf16[56,192,192]{2,1,0:T(8,128)(2,1)} %param.8), kind=kOutput, calls=%fused_computation.35 | convolution fusion | flops 264241152 | bytes 8257536 | tf_op jit(solution)/shard_map/bpj,bij->bpi/dot_general | solution.py:20
  30.7 3.3 %reshape.7 = f32[56,12288]{1,0:T(8,128)S(1)} reshape(f32[56,64,192]{2,1,0:T(8,128)} %fusion.9) | data formatting | bytes 5505024 | tf_op jit(solution)/shard_map/reshape | solution.py:24
  34.0 0.0 copy-start.1
  34.0 3.5 %dot_general.17 = f32[64,192,56]{1,0,2:T(8,128)} reshape(f32[12288,56]{0,1:T(8,128)S(1)} %bitcast.19) | data formatting | bytes 5505024 | tf_op jit(solution)/shard_map/dot_general | solution.py:24
  37.5 0.0 copy-done.1
  37.5 0.0 copy-start
  37.5 5.9 %fusion = bf16[8,64,192]{2,0,1:T(8,128)(2,1)S(1)} fusion(f32[64,192,56]{1,0,2:T(8,128)} %dot_general.17, f32[56]{0:T(128)S(1)} %compare_select_fusion.5, s32[56]{0:T(128)S(1)} %copy-done.1), kind=kOutput, calls=%fused_computation.5 | convolution fusion | flops 66061184 | bytes 2949568 | tf_op jit(solution)/shard_map/dot_general | solution.py:24
  43.4 2.2 %all_gather.3 = bf16[8,128,192]{2,1,0:T(8,128)(2,1)S(1)} all-gather(bf16[8,64,192]{2,1,0:T(8,128)(2,1)S(1)} %copy.17), channel_id=1, replica_groups=mesh['mesh'=16,'panel'=2] {'panel'}, dimensions={1}, use_global_device_ids=true | all-gather | bytes 589824 | tf_op jit(solution)/shard_map/all_gather | solution.py:42
  45.6 0.0 copy-done
  45.6 0.3 convolution_bitcast_fusion
  45.9 72.7 %all-reduce = f32[64,128]{1,0:T(8,128)S(1)} all-reduce(f32[64,128]{1,0:T(8,128)S(1)} %convolution_bitcast_fusion), channel_id=2, replica_groups=mesh['mesh'=16,'panel'=2] {'mesh'}, use_global_device_ids=true, to_apply=%region_0.1.clone | all-reduce | flops 8192 | bytes 65536
  118.6 0.1 constant_dynamic-slice_fusion
  118.7 0.7 copy.9
  (10 shorter events, 0.1 us)
Async XLA Ops:
  2.4 21.3 %collective-permute-start = (bf16[4,64,192]{2,1,0:T(8,128)(2,1)S(1)}, bf16[4,64,192]{2,1,0:T(8,128)(2,1)S(1)}, u32[]{:S(2)}, u32[]{:S(2)}) collective-permute-start(bf16[4,64,192]{2,1,0:T(8,128)(2,1)S(1)} %gather_fusion), channel_id=1, source_target_pairs={{30,0},{0,2},{2,4},{4,6},{6,8},{8,10},{10,12},{12,14},{14,16},{16,... | collective-permute-start | bytes 294920 | tf_op jit(solution)/shard_map/ppermute | solution.py:15
  6.9 16.8 %collective-permute-start.1 = (bf16[4,64,192]{2,1,0:T(8,128)(2,1)S(1)}, bf16[4,64,192]{2,1,0:T(8,128)(2,1)S(1)}, u32[]{:S(2)}, u32[]{:S(2)}) collective-permute-start(bf16[4,64,192]{2,1,0:T(8,128)(2,1)S(1)} %gather_fusion.1), channel_id=1, source_target_pairs={{2,0},{4,2},{6,4},{8,6},{10,8},{12,10},{14,12},{16,14},{18,16},{20... | collective-permute-start | bytes 294920 | tf_op jit(solution)/shard_map/ppermute | solution.py:15
  12.5 11.3 %collective-permute-start.2 = (bf16[4,64,192]{2,1,0:T(8,128)(2,1)S(1)}, bf16[4,64,192]{2,1,0:T(8,128)(2,1)S(1)}, u32[]{:S(2)}, u32[]{:S(2)}) collective-permute-start(bf16[4,64,192]{2,1,0:T(8,128)(2,1)S(1)} %gather_fusion.2), channel_id=1, source_target_pairs={{28,0},{30,2},{0,4},{2,6},{4,8},{6,10},{8,12},{10,14},{12,16},{14,... | collective-permute-start | bytes 294920 | tf_op jit(solution)/shard_map/ppermute | solution.py:15
  14.1 9.7 %collective-permute-start.3 = (bf16[4,64,192]{2,1,0:T(8,128)(2,1)S(1)}, bf16[4,64,192]{2,1,0:T(8,128)(2,1)S(1)}, u32[]{:S(2)}, u32[]{:S(2)}) collective-permute-start(bf16[4,64,192]{2,1,0:T(8,128)(2,1)S(1)} %gather_fusion.3), channel_id=1, source_target_pairs={{4,0},{6,2},{8,4},{10,6},{12,8},{14,10},{16,12},{18,14},{20,16},{2... | collective-permute-start | bytes 294920 | tf_op jit(solution)/shard_map/ppermute | solution.py:15
  34.0 3.5 %copy-start.1 = (s32[56]{0:T(128)S(1)}, s32[56]{0:T(128)}, u32[]{:S(2)}) copy-start(s32[56]{0:T(128)} %param.9) | copy-start | bytes 676
  37.5 8.1 %copy-start = (bf16[8,64,192]{2,1,0:T(8,128)(2,1)S(1)}, bf16[8,64,192]{2,1,0:T(8,128)(2,1)}, u32[]{:S(2)}) copy-start(bf16[8,64,192]{2,1,0:T(8,128)(2,1)} %param.7) | copy-start | bytes 589828
where the time goes:
time: 120 us; the launch traced here: 119 us
  blocking collectives  74.9 us (62%)
  local copies, waits for them, and re-layouts  16.5 us (14%)
  matrix products  12.4 us (10%)
  starting transfers between devices  11.9 us (10%)
  other arithmetic  2.23 us (2%)
  between operations  1.49 us (1%)
    unnamed x1, blocking collectives  72.7 us
    ppermute x4, starting transfers between devices, passed_along(): return lax.ppermute(block, axis, route)  11.9 us
    dot_general x1, matrix products, group_term(): jnp.einsum('bpj,bij->bpi', sources, blocks_here, preferred_element_type=j...  6.22 us
    gather x4, local copies, waits for them, and re-layouts, local(): picked = basis_vectors[listed]  6.02 us
    dot_general x1, matrix products, group_term(): jnp.dot(selector, product.reshape(product.shape[0], -1), precision=lax.Pr...  5.87 us
    dot_general x2, local copies, waits for them, and re-layouts, group_term(): jnp.dot(selector, product.reshape(product.shape[0], -1), precision=lax.Pr...  3.53 us
    reshape x1, local copies, waits for them, and re-layouts, group_term(): product.reshape(product.shape[0], -1)  3.3 us
  transfers between devices with their start and end apart: 4, of which 0 were waited for; matrix products, arithmetic and copies ran while one was open for 7% of the time, Pallas kernels for 0%

commit v1 on v0

--- a/solution.py
+++ b/solution.py
@@ -1,12 +1,18 @@
+import functools
+
 import jax
 import jax.numpy as jnp
 from jax import lax
+from jax.experimental import pallas as pl
+from jax.experimental.pallas import tpu as pltpu
 from jax.sharding import PartitionSpec as P
 
 GMAX = 4
-
-
-neighbour_offsets = (1, -1, 2, -2)
+OFFSETS = (1, -1, 2, -2)
+NEIGH = len(OFFSETS)
+MESH = pl.DeviceIdType.MESH
+UNROLL = 8
+K_PARTS = 4
 
 
 def passed_along(block, axis, distance):
@@ -24,13 +30,13 @@
     return jnp.dot(selector, product.reshape(product.shape[0], -1), precision=lax.Precision.HIGHEST)
 
 
-def local(
+def generic_local(
     basis_vectors, stiffness_blocks, block_rows, block_columns, density, block_counts, send_list
 ):
     clusters, panel_width, cluster_dofs = basis_vectors.shape
     capacity = stiffness_blocks.shape[0]
     arriving = []
-    for neighbour, offset in enumerate(neighbour_offsets):
+    for neighbour, offset in enumerate(OFFSETS):
         listed = send_list[neighbour * GMAX : (neighbour + 1) * GMAX]
         picked = basis_vectors[listed]
         arriving.append(passed_along(picked, "mesh", offset))
@@ -46,6 +52,272 @@
     return lax.psum_scatter(partial_tile, "mesh", scatter_dimension=1, tiled=True)
 
 
+def kernel(
+    n_mesh,
+    rows_s,
+    cols_s,
+    dens_s,
+    count_s,
+    send_s,
+    cols_v,
+    basis_hbm,
+    k_hbm,
+    out_ref,
+    v_full,
+    v_own,
+    own_packed,
+    send_buf,
+    ghost,
+    k_v,
+    prefix,
+    w2,
+    part,
+    landed,
+    order_v,
+    order_s,
+    k_sem,
+    local_sem,
+    panel_send,
+    panel_recv,
+    ghost_send,
+    ghost_recv,
+    tile_send,
+    tile_recv,
+):
+    del cols_s
+    clusters, width, dofs = basis_hbm.shape
+    capacity = k_hbm.shape[0]
+    ranks = 2 * width
+    pools = clusters + NEIGH * GMAX
+    per_panel = n_mesh // 2
+    q = lax.axis_index("mesh")
+    p = lax.axis_index("panel")
+    me = q * 2 + p
+    everyone = n_mesh * 2
+
+    barrier = pltpu.get_barrier_semaphore()
+    for step in range(1, everyone):
+        other = lax.rem(me + step, everyone)
+        pl.semaphore_signal(
+            barrier, inc=1, device_id=(other // 2, lax.rem(other, 2)), device_id_type=MESH
+        )
+
+    own_rows = pl.ds(pl.multiple_of(p * width, width), width)
+    fetch_own = pltpu.make_async_copy(basis_hbm, v_own, local_sem.at[0])
+    fetch_own.start()
+    fetch_half = pltpu.make_async_copy(basis_hbm, v_full.at[:, own_rows, :], local_sem.at[1])
+    fetch_half.start()
+    piece = capacity // K_PARTS
+    fetch_k = [
+        pltpu.make_async_copy(
+            k_hbm.at[pl.ds(i * piece, piece)], k_v.at[pl.ds(i * piece, piece)], k_sem.at[i]
+        )
+        for i in range(K_PARTS)
+    ]
+    for copy in fetch_k:
+        copy.start()
+
+    lane = lax.broadcasted_iota(jnp.int32, (capacity, 128), 1)
+    sub = lax.broadcasted_iota(jnp.int32, (capacity, 128), 0)
+    columns = jnp.broadcast_to(cols_v[...], (capacity, 128))
+    keys = columns * 128 + lane
+    key_col = jnp.sum(jnp.where(lane == sub, keys, 0), axis=1, keepdims=True)
+    rank = jnp.sum(
+        jnp.where((keys < key_col) & (lane < capacity), 1, 0), axis=1, keepdims=True
+    )
+    order_v[...] = jnp.zeros_like(order_v)
+    order_v[0:1, :] = jnp.sum(jnp.where(rank == lane, sub, 0), axis=0, keepdims=True)
+    order_v[1:2, :] = jnp.sum(
+        jnp.where(key_col < (lane + 1) * 128, 1, 0), axis=0, keepdims=True
+    )
+    order_copy = pltpu.make_async_copy(order_v, order_s, local_sem.at[2])
+    order_copy.start()
+
+    fetch_own.wait()
+    for k in range(NEIGH):
+        for g in range(GMAX):
+            listed = send_s[k * GMAX + g]
+            send_buf[k, :, g * dofs : (g + 1) * dofs] = v_own[listed]
+
+    pl.semaphore_wait(barrier, everyone - 1)
+
+    to_panel = pltpu.make_async_remote_copy(
+        src_ref=basis_hbm,
+        dst_ref=v_full.at[:, own_rows, :],
+        send_sem=panel_send,
+        recv_sem=panel_recv,
+        device_id=(q, 1 - p),
+        device_id_type=MESH,
+    )
+    to_panel.start()
+    ghosts = []
+    for k, offset in enumerate(OFFSETS):
+        copy = pltpu.make_async_remote_copy(
+            src_ref=send_buf.at[k],
+            dst_ref=ghost.at[k],
+            send_sem=ghost_send.at[k],
+            recv_sem=ghost_recv.at[k],
+            device_id=(lax.rem(q + offset + n_mesh, n_mesh), p),
+            device_id_type=MESH,
+        )
+        copy.start()
+        ghosts.append(copy)
+
+    for s in range(clusters):
+        own_packed[:, s * dofs : (s + 1) * dofs] = v_own[s]
+
+    order_copy.wait()
+    fetch_half.wait()
+    for copy in fetch_k:
+        copy.wait()
+    to_panel.wait_recv()
+
+    count = count_s[0]
+    prefix[0] = jnp.zeros((ranks, dofs), jnp.float32)
+
+    def several(t, carry):
+        total = prefix[t * UNROLL]
+        for u in range(UNROLL):
+            at = t * UNROLL + u
+            b = order_s[0, at]
+            d = dens_s[b]
+            scale = jnp.where(b < count, 0.001 + d * d * d, jnp.float32(0.0))
+            term = jnp.dot(v_full[rows_s[b]], k_v[b], preferred_element_type=jnp.float32)
+            total = total + scale * term
+            prefix[at + 1] = total
+        return carry
+
+    lax.fori_loop(0, capacity // UNROLL, several, 0)
+
+    for s in range(pools):
+        w = prefix[order_s[1, s]]
+        if s > 0:
+            w = w - prefix[order_s[1, s - 1]]
+        high = w.astype(jnp.bfloat16)
+        w2[0:ranks, s * dofs : (s + 1) * dofs] = high
+        w2[ranks : 2 * ranks, s * dofs : (s + 1) * dofs] = (
+            w - high.astype(jnp.float32)
+        ).astype(jnp.bfloat16)
+
+    def against(slabs, first, length):
+        return lax.dot_general(
+            slabs,
+            w2[:, first : first + length],
+            (((1,), (1,)), ((), ())),
+            preferred_element_type=jnp.float32,
+        )
+
+    both = against(own_packed[...], 0, clusters * dofs)
+    for k in range(NEIGH):
+        ghosts[k].wait_recv()
+        both = both + against(ghost[k], (clusters + k * GMAX) * dofs, GMAX * dofs)
+    whole = both[:, :ranks] + both[:, ranks:]
+    for j in range(per_panel):
+        part[j] = whole[j * 8 : (j + 1) * 8]
+
+    tiles = []
+    for j in range(per_panel):
+        for half in range(2):
+            target = p * per_panel + j
+            tiles.append(
+                (
+                    (target == q) & (p == half),
+                    pltpu.make_async_remote_copy(
+                        src_ref=part.at[j],
+                        dst_ref=landed.at[q],
+                        send_sem=tile_send.at[j * 2 + half],
+                        recv_sem=tile_recv.at[q],
+                        device_id=(target, half),
+                        device_id_type=MESH,
+                    ),
+                    pltpu.make_async_copy(part.at[j], landed.at[q], tile_recv.at[q]),
+                )
+            )
+    for own, remote, local in tiles:
+
+        @pl.when(jnp.logical_not(own))
+        def _():
+            remote.start()
+
+        @pl.when(own)
+        def _():
+            local.start()
+
+    to_panel.wait_send()
+    for copy in ghosts:
+        copy.wait_send()
+
+    for source in range(n_mesh):
+        pltpu.make_async_copy(part.at[0], landed.at[source], tile_recv.at[source]).wait()
+    total = landed[0]
+    for source in range(1, n_mesh):
+        total = total + landed[source]
+    turned = total.T
+    out_ref[...] = jnp.where(p == 0, turned[:width], turned[width:])
+
+    for own, remote, local in tiles:
+
+        @pl.when(jnp.logical_not(own))
+        def _():
+            remote.wait_send()
+
+
+def fused_local(
+    basis_vectors, stiffness_blocks, block_rows, block_columns, density, block_counts, send_list
+):
+    clusters, width, dofs = basis_vectors.shape
+    capacity = stiffness_blocks.shape[0]
+    n_mesh = lax.axis_size("mesh")
+    ranks = 2 * width
+    pools = clusters + NEIGH * GMAX
+    tile = ranks // n_mesh
+    cols_row = jnp.pad(block_columns, (0, 128 - capacity)).reshape(1, 128)
+    smem = pl.BlockSpec(memory_space=pltpu.SMEM)
+    vmem = pl.BlockSpec(memory_space=pltpu.VMEM)
+    anywhere = pl.BlockSpec(memory_space=pl.ANY)
+    dma = pltpu.SemaphoreType.DMA
+    return pl.pallas_call(
+        functools.partial(kernel, n_mesh),
+        out_shape=jax.ShapeDtypeStruct((width, tile), jnp.float32),
+        in_specs=[smem] * 5 + [vmem, anywhere, anywhere],
+        out_specs=vmem,
+        scratch_shapes=[
+            pltpu.VMEM((clusters, ranks, dofs), jnp.bfloat16),
+            pltpu.VMEM((clusters, width, dofs), jnp.bfloat16),
+            pltpu.VMEM((width, clusters * dofs), jnp.bfloat16),
+            pltpu.VMEM((NEIGH, width, GMAX * dofs), jnp.bfloat16),
+            pltpu.VMEM((NEIGH, width, GMAX * dofs), jnp.bfloat16),
+            pltpu.VMEM((capacity, dofs, dofs), jnp.bfloat16),
+            pltpu.VMEM((capacity + 1, ranks, dofs), jnp.float32),
+            pltpu.VMEM((2 * ranks, pools * dofs), jnp.bfloat16),
+            pltpu.VMEM((n_mesh // 2, tile, ranks), jnp.float32),
+            pltpu.VMEM((n_mesh, tile, ranks), jnp.float32),
+            pltpu.VMEM((8, 128), jnp.int32),
+            pltpu.SMEM((8, 128), jnp.int32),
+            dma((K_PARTS,)),
+            dma((3,)),
+            dma,
+            dma,
+            dma((NEIGH,)),
+            dma((NEIGH,)),
+            dma((n_mesh,)),
+            dma((n_mesh,)),
+        ],
+        compiler_params=pltpu.CompilerParams(
+            collective_id=0, has_side_effects=True, vmem_limit_bytes=40 * 1024 * 1024
+        ),
+    )(
+        block_rows,
+        block_columns,
+        density,
+        block_counts,
+        send_list,
+        cols_row,
+        basis_vectors,
+        stiffness_blocks,
+    )
+
+
 def solution(mesh):
     placed = (
         P("mesh", "panel", None),
@@ -56,6 +328,19 @@
         P("mesh"),
         P("mesh"),
     )
-    return jax.shard_map(
-        local, mesh=mesh, in_specs=placed, out_specs=P("panel", "mesh"), check_vma=False
-    )
+    fused = jax.shard_map(
+        fused_local, mesh=mesh, in_specs=placed, out_specs=P("panel", "mesh"), check_vma=False
+    )
+    generic = jax.shard_map(
+        generic_local, mesh=mesh, in_specs=placed, out_specs=P("panel", "mesh"), check_vma=False
+    )
+
+    def run(basis_vectors, stiffness_blocks, *rest):
+        n_mesh, n_panel = mesh.shape["mesh"], mesh.shape["panel"]
+        ranks = basis_vectors.shape[1]
+        capacity = stiffness_blocks.shape[0] // n_mesh
+        fits = n_panel == 2 and ranks == 128 and ranks == 8 * n_mesh
+        fits = fits and capacity % UNROLL == 0 and capacity <= 128
+        return (fused if fits else generic)(basis_vectors, stiffness_blocks, *rest)
+
+    return run

time: 120 us -> 28.9 us (0.24)
  blocking collectives: 74.9 us -> 0 us
  Pallas kernels: 0 us -> 20.5 us
  matrix products: 12.4 us -> 0 us
  starting transfers between devices: 11.9 us -> 0 us
  local copies, waits for them, and re-layouts: 16.5 us -> 7.45 us
  other arithmetic: 2.23 us -> 0 us
    unnamed x1 -> x0, blocking collectives: 72.7 us -> none
    pallas_call x0 -> x1, Pallas kernels: none -> 20.5 us  [fused_local(): pl.pallas_call(functools.partial(kernel, n_mesh), out_shape=jax.ShapeDtyp...]
    dot_general x3 -> x0, matrix products: 12.4 us -> none  [the longest x1 6.22 us: group_term(): jnp.einsum('bpj,bij->bpi', sources, blocks_here, preferred_element_type=j...]
    ppermute x4 -> x0, starting transfers between devices: 11.9 us -> none  [passed_along(): return lax.ppermute(block, axis, route)]
    gather x5 -> x0, local copies, waits for them, and re-layouts: 6.7 us -> none  [the longest x4 6.02 us: local(): picked = basis_vectors[listed]]
    unnamed x10 -> x12, local copies, waits for them, and re-layouts: 2.32 us -> 6.13 us
    dot_general x2 -> x0, local copies, waits for them, and re-layouts: 3.53 us -> none  [group_term(): jnp.dot(selector, product.reshape(product.shape[0], -1), precision=lax.Pr...]
    reshape x1, local copies, waits for them, and re-layouts: 3.3 us -> 0.66 us  [fused_local(): cols_row = jnp.pad(block_columns, (0, 128 - capacity)).reshape(1, 128)]
  transfers between devices with their start and end apart: 4 -> 0, of which waited for: 0 -> 0; matrix products, arithmetic and copies ran while one was open for 7% -> 0% of each run, Pallas kernels for 0% -> 0%
where the time goes in v1:
time: 28.9 us; the launch traced here: 28.6 us
  Pallas kernels  20.5 us (71%)
  local copies, waits for them, and re-layouts  7.45 us (26%)
  between operations  0.67 us (2%)
    pallas_call x1, Pallas kernels, fused_local(): pl.pallas_call(functools.partial(kernel, n_mesh), out_shape=jax.ShapeDtyp...  20.5 us
    unnamed x12, local copies, waits for them, and re-layouts  6.13 us
    pallas_call x1, local copies, waits for them, and re-layouts, fused_local(): pl.pallas_call(functools.partial(kernel, n_mesh), out_shape=jax.ShapeDtyp...  0.66 us
    reshape x1, local copies, waits for them, and re-layouts, fused_local(): cols_row = jnp.pad(block_columns, (0, 128 - capacity)).reshape(1, 128)  0.66 us

profile of v1, /device:TPU:0, one launch (start us, length us, event | category | flops | bytes accessed | tf_op | source)
XLA Modules:
  0.0 28.6 jit_solution(7317023251198659512)
XLA Ops:
  0.7 0.7 %pad_bitcast_fusion.cols_v = s32[1,128]{1,0:T(1,128)S(1)} fusion(s32[56]{0:T(128)} %cols_s.1), kind=kLoop, calls=%fused_computation | loop fusion | bytes 736 | tf_op jit(solution)/shard_map/reshape | solution.py:274
  1.3 0.0 copy-start
  1.3 2.6 %copy-done = bf16[56,192,192]{2,1,0:T(8,128)(2,1)S(1)} copy-done((bf16[56,192,192]{2,1,0:T(8,128)(2,1)S(1)}, bf16[56,192,192]{2,1,0:T(8,128)(2,1)}, u32[]{:S(2)}) %copy-start) | copy-done | bytes 4128792
  3.9 0.0 copy-start.1
  3.9 0.9 %copy-done.1 = bf16[8,64,192]{2,1,0:T(8,128)(2,1)S(1)} copy-done((bf16[8,64,192]{2,1,0:T(8,128)(2,1)S(1)}, bf16[8,64,192]{2,1,0:T(8,128)(2,1)}, u32[]{:S(2)}) %copy-start.1) | copy-done | bytes 196632
  4.8 0.0 copy-start.2
  4.8 0.7 %copy-done.2 = s32[56]{0:T(128)S(1)} copy-done((s32[56]{0:T(128)S(1)}, s32[56]{0:T(128)}, u32[]{:S(2)}) %copy-start.2) | copy-done | bytes 248
  5.5 0.0 copy-start.3
  5.5 0.7 %copy-done.3 = s32[56]{0:T(128)S(1)} copy-done((s32[56]{0:T(128)S(1)}, s32[56]{0:T(128)}, u32[]{:S(2)}) %copy-start.3) | copy-done | bytes 248
  6.1 0.0 copy-start.4
  6.1 0.7 %copy-done.4 = f32[56]{0:T(128)S(1)} copy-done((f32[56]{0:T(128)S(1)}, f32[56]{0:T(128)}, u32[]{:S(2)}) %copy-start.4) | copy-done | bytes 248
  6.8 0.0 copy-start.5
  6.8 0.7 %copy-done.5 = s32[16]{0:T(128)S(1)} copy-done((s32[16]{0:T(128)S(1)}, s32[16]{0:T(128)}, u32[]{:S(2)}) %copy-start.5) | copy-done | bytes 88
  7.4 20.5 %shard_map.73 = f32[64,8]{1,0:T(8,128)S(1)} custom-call(s32[56]{0:T(128)S(1)} %copy-done.2, s32[56]{0:T(128)S(1)} %copy-done.3, f32[56]{0:T(128)S(1)} %copy-done.4, s32[1]{0:T(128)S(6)} %copy.9.count_s, s32[16]{0:T(128)S(1)} %copy-done.5, s32[1,128]{1,0:T(1,128)S(1)} %pad_bitcast_fusion.cols_v, bf16[8,64,192]{2,1,0:T(8,128)(2,1)S(1)} %copy-done.1, ...), custom_call_target="tpu_custom_call" | custom-call | tf_op jit(solution)/shard_map/pallas_call | solution.py:279
  28.0 0.7 %copy.8 = f32[64,8]{0,1:T(8,128)} copy(f32[64,8]{1,0:T(8,128)S(1)} %shard_map.73) | data formatting | bytes 4096 | tf_op jit(solution)/shard_map/pallas_call | solution.py:279
Async XLA Ops:
  1.3 2.6 %copy-start = (bf16[56,192,192]{2,1,0:T(8,128)(2,1)S(1)}, bf16[56,192,192]{2,1,0:T(8,128)(2,1)}, u32[]{:S(2)}) copy-start(bf16[56,192,192]{2,1,0:T(8,128)(2,1)} %k_hbm.1) | copy-start | bytes 12386308
  3.9 0.9 %copy-start.1 = (bf16[8,64,192]{2,1,0:T(8,128)(2,1)S(1)}, bf16[8,64,192]{2,1,0:T(8,128)(2,1)}, u32[]{:S(2)}) copy-start(bf16[8,64,192]{2,1,0:T(8,128)(2,1)} %basis_hbm.1) | copy-start | bytes 589828
  4.8 0.7 %copy-start.2 = (s32[56]{0:T(128)S(1)}, s32[56]{0:T(128)}, u32[]{:S(2)}) copy-start(s32[56]{0:T(128)} %rows_s.1) | copy-start | bytes 676
  5.5 0.7 %copy-start.3 = (s32[56]{0:T(128)S(1)}, s32[56]{0:T(128)}, u32[]{:S(2)}) copy-start(s32[56]{0:T(128)} %cols_s.1) | copy-start | bytes 676
  6.1 0.7 %copy-start.4 = (f32[56]{0:T(128)S(1)}, f32[56]{0:T(128)}, u32[]{:S(2)}) copy-start(f32[56]{0:T(128)} %dens_s.1) | copy-start | bytes 676
  6.8 0.7 %copy-start.5 = (s32[16]{0:T(128)S(1)}, s32[16]{0:T(128)}, u32[]{:S(2)}) copy-start(s32[16]{0:T(128)} %send_s.1) | copy-start | bytes 196

commit v2 on v1

--- a/solution.py
+++ b/solution.py
@@ -54,15 +54,19 @@
 
 def kernel(
     n_mesh,
+    rows_hbm,
+    cols_hbm,
+    dens_hbm,
+    count_hbm,
+    send_hbm,
+    basis_hbm,
+    k_hbm,
+    out_ref,
     rows_s,
     cols_s,
     dens_s,
     count_s,
     send_s,
-    cols_v,
-    basis_hbm,
-    k_hbm,
-    out_ref,
     v_full,
     v_own,
     own_packed,
@@ -84,7 +88,6 @@
     tile_send,
     tile_recv,
 ):
-    del cols_s
     clusters, width, dofs = basis_hbm.shape
     capacity = k_hbm.shape[0]
     ranks = 2 * width
@@ -102,6 +105,20 @@
             barrier, inc=1, device_id=(other // 2, lax.rem(other, 2)), device_id_type=MESH
         )
 
+    lists = [
+        pltpu.make_async_copy(source, held, local_sem.at[3 + i])
+        for i, (source, held) in enumerate(
+            (
+                (send_hbm, send_s),
+                (cols_hbm, cols_s),
+                (rows_hbm, rows_s),
+                (dens_hbm, dens_s),
+                (count_hbm, count_s),
+            )
+        )
+    ]
+    for copy in lists:
+        copy.start()
     own_rows = pl.ds(pl.multiple_of(p * width, width), width)
     fetch_own = pltpu.make_async_copy(basis_hbm, v_own, local_sem.at[0])
     fetch_own.start()
@@ -117,21 +134,8 @@
     for copy in fetch_k:
         copy.start()
 
-    lane = lax.broadcasted_iota(jnp.int32, (capacity, 128), 1)
-    sub = lax.broadcasted_iota(jnp.int32, (capacity, 128), 0)
-    columns = jnp.broadcast_to(cols_v[...], (capacity, 128))
-    keys = columns * 128 + lane
-    key_col = jnp.sum(jnp.where(lane == sub, keys, 0), axis=1, keepdims=True)
-    rank = jnp.sum(
-        jnp.where((keys < key_col) & (lane < capacity), 1, 0), axis=1, keepdims=True
-    )
-    order_v[...] = jnp.zeros_like(order_v)
-    order_v[0:1, :] = jnp.sum(jnp.where(rank == lane, sub, 0), axis=0, keepdims=True)
-    order_v[1:2, :] = jnp.sum(
-        jnp.where(key_col < (lane + 1) * 128, 1, 0), axis=0, keepdims=True
-    )
-    order_copy = pltpu.make_async_copy(order_v, order_s, local_sem.at[2])
-    order_copy.start()
+    for copy in lists:
+        copy.wait()
 
     fetch_own.wait()
     for k in range(NEIGH):
@@ -142,7 +146,7 @@
     pl.semaphore_wait(barrier, everyone - 1)
 
     to_panel = pltpu.make_async_remote_copy(
-        src_ref=basis_hbm,
+        src_ref=v_own,
         dst_ref=v_full.at[:, own_rows, :],
         send_sem=panel_send,
         recv_sem=panel_recv,
@@ -162,6 +166,26 @@
         )
         copy.start()
         ghosts.append(copy)
+
+    lane = lax.broadcasted_iota(jnp.int32, (capacity, 128), 1)
+    sub = lax.broadcasted_iota(jnp.int32, (capacity, 128), 0)
+    lane_row = lax.broadcasted_iota(jnp.int32, (1, 128), 1)
+    columns = jnp.zeros((1, 128), jnp.int32)
+    for b in range(capacity):
+        columns = jnp.where(lane_row == b, cols_s[b], columns)
+    columns = jnp.broadcast_to(columns, (capacity, 128))
+    keys = columns * 128 + lane
+    key_col = jnp.sum(jnp.where(lane == sub, keys, 0), axis=1, keepdims=True)
+    rank = jnp.sum(
+        jnp.where((keys < key_col) & (lane < capacity), 1, 0), axis=1, keepdims=True
+    )
+    order_v[...] = jnp.zeros_like(order_v)
+    order_v[0:1, :] = jnp.sum(jnp.where(rank == lane, sub, 0), axis=0, keepdims=True)
+    order_v[1:2, :] = jnp.sum(
+        jnp.where(key_col < (lane + 1) * 128, 1, 0), axis=0, keepdims=True
+    )
+    order_copy = pltpu.make_async_copy(order_v, order_s, local_sem.at[2])
+    order_copy.start()
 
     for s in range(clusters):
         own_packed[:, s * dofs : (s + 1) * dofs] = v_own[s]
@@ -212,8 +236,14 @@
         ghosts[k].wait_recv()
         both = both + against(ghost[k], (clusters + k * GMAX) * dofs, GMAX * dofs)
     whole = both[:, :ranks] + both[:, ranks:]
+    tall = lax.broadcasted_iota(jnp.int32, (8, ranks), 0)
+    wide = lax.broadcasted_iota(jnp.int32, (8, ranks), 1)
     for j in range(per_panel):
-        part[j] = whole[j * 8 : (j + 1) * 8]
+        tile = whole[j * 8 : (j + 1) * 8]
+        crossed = pltpu.roll(pltpu.roll(tile, 4, 0), width, 1)
+        tile = jnp.where((wide < width) == (tall < 4), tile, crossed)
+        part[j, 0] = tile[:4]
+        part[j, 1] = tile[4:]
 
     tiles = []
     for j in range(per_panel):
@@ -223,14 +253,14 @@
                 (
                     (target == q) & (p == half),
                     pltpu.make_async_remote_copy(
-                        src_ref=part.at[j],
+                        src_ref=part.at[j, half],
                         dst_ref=landed.at[q],
                         send_sem=tile_send.at[j * 2 + half],
                         recv_sem=tile_recv.at[q],
                         device_id=(target, half),
                         device_id_type=MESH,
                     ),
-                    pltpu.make_async_copy(part.at[j], landed.at[q], tile_recv.at[q]),
+                    pltpu.make_async_copy(part.at[j, half], landed.at[q], tile_recv.at[q]),
                 )
             )
     for own, remote, local in tiles:
@@ -248,12 +278,12 @@
         copy.wait_send()
 
     for source in range(n_mesh):
-        pltpu.make_async_copy(part.at[0], landed.at[source], tile_recv.at[source]).wait()
+        pltpu.make_async_copy(part.at[0, 0], landed.at[source], tile_recv.at[source]).wait()
     total = landed[0]
     for source in range(1, n_mesh):
         total = total + landed[source]
-    turned = total.T
-    out_ref[...] = jnp.where(p == 0, turned[:width], turned[width:])
+    out_ref[0:4, :] = total[:, :width]
+    out_ref[4:8, :] = total[:, width:]
 
     for own, remote, local in tiles:
 
@@ -271,17 +301,20 @@
     ranks = 2 * width
     pools = clusters + NEIGH * GMAX
     tile = ranks // n_mesh
-    cols_row = jnp.pad(block_columns, (0, 128 - capacity)).reshape(1, 128)
-    smem = pl.BlockSpec(memory_space=pltpu.SMEM)
+    in_hbm = pl.BlockSpec(memory_space=pltpu.HBM)
     vmem = pl.BlockSpec(memory_space=pltpu.VMEM)
-    anywhere = pl.BlockSpec(memory_space=pl.ANY)
     dma = pltpu.SemaphoreType.DMA
-    return pl.pallas_call(
+    turned = pl.pallas_call(
         functools.partial(kernel, n_mesh),
-        out_shape=jax.ShapeDtypeStruct((width, tile), jnp.float32),
-        in_specs=[smem] * 5 + [vmem, anywhere, anywhere],
+        out_shape=jax.ShapeDtypeStruct((tile, width), jnp.float32),
+        in_specs=[in_hbm] * 7,
         out_specs=vmem,
         scratch_shapes=[
+            pltpu.SMEM((capacity,), jnp.int32),
+            pltpu.SMEM((capacity,), jnp.int32),
+            pltpu.SMEM((capacity,), jnp.float32),
+            pltpu.SMEM((1,), jnp.int32),
+            pltpu.SMEM((NEIGH * GMAX,), jnp.int32),
             pltpu.VMEM((clusters, ranks, dofs), jnp.bfloat16),
             pltpu.VMEM((clusters, width, dofs), jnp.bfloat16),
             pltpu.VMEM((width, clusters * dofs), jnp.bfloat16),
@@ -290,12 +323,12 @@
             pltpu.VMEM((capacity, dofs, dofs), jnp.bfloat16),
             pltpu.VMEM((capacity + 1, ranks, dofs), jnp.float32),
             pltpu.VMEM((2 * ranks, pools * dofs), jnp.bfloat16),
-            pltpu.VMEM((n_mesh // 2, tile, ranks), jnp.float32),
-            pltpu.VMEM((n_mesh, tile, ranks), jnp.float32),
+            pltpu.VMEM((n_mesh // 2, 2, tile // 2, ranks), jnp.float32),
+            pltpu.VMEM((n_mesh, tile // 2, ranks), jnp.float32),
             pltpu.VMEM((8, 128), jnp.int32),
             pltpu.SMEM((8, 128), jnp.int32),
             dma((K_PARTS,)),
-            dma((3,)),
+            dma((8,)),
             dma,
             dma,
             dma((NEIGH,)),
@@ -304,7 +337,7 @@
             dma((n_mesh,)),
         ],
         compiler_params=pltpu.CompilerParams(
-            collective_id=0, has_side_effects=True, vmem_limit_bytes=40 * 1024 * 1024
+            collective_id=0, has_side_effects=True, vmem_limit_bytes=63 * 1024 * 1024
         ),
     )(
         block_rows,
@@ -312,10 +345,10 @@
         density,
         block_counts,
         send_list,
-        cols_row,
         basis_vectors,
         stiffness_blocks,
     )
+    return turned.T
 
 
 def solution(mesh):

time: 28.9 us -> 22.7 us (0.79)
  local copies, waits for them, and re-layouts: 7.45 us -> 1.28 us
    unnamed x12 -> x1, local copies, waits for them, and re-layouts: 6.13 us -> 1.28 us
    pallas_call x1 -> x0, local copies, waits for them, and re-layouts: 0.66 us -> none  [fused_local(): pl.pallas_call(functools.partial(kernel, n_mesh), out_shape=jax.ShapeDtyp...]
    reshape x1 -> x0, local copies, waits for them, and re-layouts: 0.66 us -> none  [fused_local(): cols_row = jnp.pad(block_columns, (0, 128 - capacity)).reshape(1, 128)]
where the time goes in v2:
time: 22.7 us; the launch traced here: 22.6 us
  Pallas kernels  20.6 us (91%)
  local copies, waits for them, and re-layouts  1.28 us (6%)
  between operations  0.66 us (3%)
    pallas_call x1, Pallas kernels, fused_local(): pl.pallas_call(functools.partial(kernel, n_mesh), out_shape=jax.ShapeDtyp...  20.6 us
    unnamed x1, local copies, waits for them, and re-layouts  1.28 us

profile of v2, /device:TPU:0, one launch (start us, length us, event | category | flops | bytes accessed | tf_op | source)
XLA Modules:
  0.0 22.6 jit_solution(14939180711550393786)
XLA Ops:
  0.7 20.6 %shard_map.73 = f32[8,64]{1,0:T(8,128)} custom-call(s32[56]{0:T(128)} %rows_hbm.1, s32[56]{0:T(128)} %cols_hbm.1, f32[56]{0:T(128)} %dens_hbm.1, s32[1]{0:T(128)S(6)} %copy.9.count_hbm, s32[16]{0:T(128)} %send_hbm.1, bf16[8,64,192]{2,1,0:T(8,128)(2,1)} %basis_hbm.1, bf16[56,192,192]{2,1,0:T(8,128)(2,1)} %k_hbm.1), custom_call_target="tpu_custom_call" | custom-call | tf_op jit(solution)/shard_map/pallas_call | solution.py:307
  21.3 1.3 %copy.10 = f32[64,8]{0,1:T(8,128)} copy(f32[64,8]{0,1:T(8,128)} %bitcast.1) | data formatting | bytes 4096

commit v3 on v2

--- a/solution.py
+++ b/solution.py
@@ -11,7 +11,7 @@
 OFFSETS = (1, -1, 2, -2)
 NEIGH = len(OFFSETS)
 MESH = pl.DeviceIdType.MESH
-UNROLL = 8
+UNROLL = 14
 K_PARTS = 4
 
 
@@ -98,13 +98,6 @@
     me = q * 2 + p
     everyone = n_mesh * 2
 
-    barrier = pltpu.get_barrier_semaphore()
-    for step in range(1, everyone):
-        other = lax.rem(me + step, everyone)
-        pl.semaphore_signal(
-            barrier, inc=1, device_id=(other // 2, lax.rem(other, 2)), device_id_type=MESH
-        )
-
     lists = [
         pltpu.make_async_copy(source, held, local_sem.at[3 + i])
         for i, (source, held) in enumerate(
@@ -122,6 +115,14 @@
     own_rows = pl.ds(pl.multiple_of(p * width, width), width)
     fetch_own = pltpu.make_async_copy(basis_hbm, v_own, local_sem.at[0])
     fetch_own.start()
+
+    barrier = pltpu.get_barrier_semaphore()
+    for step in range(1, everyone):
+        other = lax.rem(me + step, everyone)
+        pl.semaphore_signal(
+            barrier, inc=1, device_id=(other // 2, lax.rem(other, 2)), device_id_type=MESH
+        )
+
     fetch_half = pltpu.make_async_copy(basis_hbm, v_full.at[:, own_rows, :], local_sem.at[1])
     fetch_half.start()
     piece = capacity // K_PARTS
@@ -134,9 +135,7 @@
     for copy in fetch_k:
         copy.start()
 
-    for copy in lists:
-        copy.wait()
-
+    lists[0].wait()
     fetch_own.wait()
     for k in range(NEIGH):
         for g in range(GMAX):
@@ -166,6 +165,9 @@
         )
         copy.start()
         ghosts.append(copy)
+
+    for copy in lists[1:]:
+        copy.wait()
 
     lane = lax.broadcasted_iota(jnp.int32, (capacity, 128), 1)
     sub = lax.broadcasted_iota(jnp.int32, (capacity, 128), 0)

time: 22.7 us -> 22.6 us (level)
  no operation moved by 1% of the time
where the time goes in v3:
time: 22.6 us; the launch traced here: 22.5 us
  Pallas kernels  20.5 us (91%)
  local copies, waits for them, and re-layouts  1.28 us (6%)
  between operations  0.66 us (3%)
    pallas_call x1, Pallas kernels, fused_local(): pl.pallas_call(functools.partial(kernel, n_mesh), out_shape=jax.ShapeDtyp...  20.5 us
    unnamed x1, local copies, waits for them, and re-layouts  1.28 us

profile of v3, /device:TPU:0, one launch (start us, length us, event | category | flops | bytes accessed | tf_op | source)
XLA Modules:
  0.0 22.5 jit_solution(3695070980678287102)
XLA Ops:
  0.7 20.5 %shard_map.73 = f32[8,64]{1,0:T(8,128)} custom-call(s32[56]{0:T(128)} %rows_hbm.1, s32[56]{0:T(128)} %cols_hbm.1, f32[56]{0:T(128)} %dens_hbm.1, s32[1]{0:T(128)S(6)} %copy.9.count_hbm, s32[16]{0:T(128)} %send_hbm.1, bf16[8,64,192]{2,1,0:T(8,128)(2,1)} %basis_hbm.1, bf16[56,192,192]{2,1,0:T(8,128)(2,1)} %k_hbm.1), custom_call_target="tpu_custom_call" | custom-call | tf_op jit(solution)/shard_map/pallas_call | solution.py:309
  21.2 1.3 %copy.10 = f32[64,8]{0,1:T(8,128)} copy(f32[64,8]{0,1:T(8,128)} %bitcast.1) | data formatting | bytes 4096

commit v4 on v3

--- a/solution.py
+++ b/solution.py
@@ -240,13 +240,6 @@
     whole = both[:, :ranks] + both[:, ranks:]
     tall = lax.broadcasted_iota(jnp.int32, (8, ranks), 0)
     wide = lax.broadcasted_iota(jnp.int32, (8, ranks), 1)
-    for j in range(per_panel):
-        tile = whole[j * 8 : (j + 1) * 8]
-        crossed = pltpu.roll(pltpu.roll(tile, 4, 0), width, 1)
-        tile = jnp.where((wide < width) == (tall < 4), tile, crossed)
-        part[j, 0] = tile[:4]
-        part[j, 1] = tile[4:]
-
     tiles = []
     for j in range(per_panel):
         for half in range(2):
@@ -265,15 +258,21 @@
                     pltpu.make_async_copy(part.at[j, half], landed.at[q], tile_recv.at[q]),
                 )
             )
-    for own, remote, local in tiles:
-
-        @pl.when(jnp.logical_not(own))
-        def _():
-            remote.start()
-
-        @pl.when(own)
-        def _():
-            local.start()
+    for j in range(per_panel):
+        tile = whole[j * 8 : (j + 1) * 8]
+        crossed = pltpu.roll(pltpu.roll(tile, 4, 0), width, 1)
+        tile = jnp.where((wide < width) == (tall < 4), tile, crossed)
+        part[j, 0] = tile[:4]
+        part[j, 1] = tile[4:]
+        for own, remote, local in tiles[2 * j : 2 * j + 2]:
+
+            @pl.when(jnp.logical_not(own))
+            def _():
+                remote.start()
+
+            @pl.when(own)
+            def _():
+                local.start()
 
     to_panel.wait_send()
     for copy in ghosts:

time: 22.6 us -> 22.6 us (level)
  no operation moved by 1% of the time
where the time goes in v4:
time: 22.6 us; the launch traced here: 22.4 us
  Pallas kernels  20.5 us (91%)
  local copies, waits for them, and re-layouts  1.28 us (6%)
  between operations  0.66 us (3%)
    pallas_call x1, Pallas kernels, fused_local(): pl.pallas_call(functools.partial(kernel, n_mesh), out_shape=jax.ShapeDtyp...  20.5 us
    unnamed x1, local copies, waits for them, and re-layouts  1.28 us

profile of v4, /device:TPU:0, one launch (start us, length us, event | category | flops | bytes accessed | tf_op | source)
XLA Modules:
  0.0 22.4 jit_solution(14763151563812471014)
XLA Ops:
  0.7 20.5 %shard_map.73 = f32[8,64]{1,0:T(8,128)} custom-call(s32[56]{0:T(128)} %rows_hbm.1, s32[56]{0:T(128)} %cols_hbm.1, f32[56]{0:T(128)} %dens_hbm.1, s32[1]{0:T(128)S(6)} %copy.9.count_hbm, s32[16]{0:T(128)} %send_hbm.1, bf16[8,64,192]{2,1,0:T(8,128)(2,1)} %basis_hbm.1, bf16[56,192,192]{2,1,0:T(8,128)(2,1)} %k_hbm.1), custom_call_target="tpu_custom_call" | custom-call | tf_op jit(solution)/shard_map/pallas_call | solution.py:308
  21.2 1.3 %copy.10 = f32[64,8]{0,1:T(8,128)} copy(f32[64,8]{0,1:T(8,128)} %bitcast.1) | data formatting | bytes 4096
